TPU v7x, 128 devices: a whole 4x4x4 slice. The times are simulated.
128 devices in a mesh: dp: 32 (over x, y, core), tp: 4 (over z).
Axes of the slice: x: 4, y: 4, z: 4, core: 2. Of those that a mesh axis runs over, the one named last changes fastest.
Arguments:
- query: bfloat16 [128, 64, 576], P('dp', 'tp'), may hold values from -65 to 65
- new_latent: bfloat16 [128, 576], P('dp'), may hold values from -4 to 4
- cache: bfloat16 [64, 1024, 576], P('dp'), may hold values from -4 to 4
- cache_len: int32 [64], P('dp'), may hold values from 128 to 1024, as said below
- w_uv: bfloat16 [64, 512, 128], P('tp'), may hold values from -1.5 to 1.5
- w_out: bfloat16 [8192, 7168], P('tp', 'dp'), may hold values from -0.0625 to 0.0625
- hidden_in: bfloat16 [128, 7168], P('tp', 'dp'), may hold values from -25 to 25
- norm_gain: float32 [7168], P('dp'), may hold values from 0.1 to 1.9
- routing: int32 [128, 8], replicated, may hold values from 0 to 15, all different within a row; in each aligned block of 32 rows (0 to 31, 32 to 63, ...) at most 24 rows name the same one
- route_weight: float32 [128, 8], replicated, may hold values from 0.1 to 0.6
- w_gate_up: bfloat16 [2, 7168, 32768], P(None, None, ('dp', 'tp')), may hold values from -0.0625 to 0.0625
- w_down: bfloat16 [32768, 7168], P(('dp', 'tp')), may hold values from -0.125 to 0.125
Outputs:
- hidden_out: bfloat16 [128, 7168], P('tp', 'dp')
Inputs may be any that keep to these rules, and one draw needn't show every extreme that they name: `routing`: each row names 8 different experts. Within each aligned block of 32 rows no expert is named by more than 24 rows, a bound that some block reaches. `cache_len`: some request holds a full cache of 1024 tokens.
All inputs are finite; a program needn't handle non-finite values.
Results may differ from a plain program's by a relative error of at most 0.006.
Values may be sent and summed in bfloat16 or wider, within the bound.
A program may use at most 128 MiB of HBM per device.

v0:
```python
import jax
import jax.numpy as jnp
import numpy as np
from jax import lax
from jax.sharding import PartitionSpec as P

D = 7168
ROPE = 64
VH = 128
EXPERTS = 16
EPSILON = 1e-06


def expert_block(tokens_in, w_gate_up, w_down):
    gate_part = jnp.dot(tokens_in, w_gate_up[0], preferred_element_type=jnp.float32)
    up_part = jnp.dot(tokens_in, w_gate_up[1], preferred_element_type=jnp.float32)
    hidden_act = (jax.nn.silu(gate_part) * up_part).astype(jnp.bfloat16)
    return jnp.dot(hidden_act, w_down, preferred_element_type=jnp.float32)


def on_device(
    query,
    new_latent,
    cache,
    cache_len,
    w_uv,
    w_out,
    hidden_in,
    norm_gain,
    routing,
    route_weight,
    w_gate_up,
    w_down,
):
    dp_count = lax.axis_size("dp")
    tp_count = lax.axis_size("tp")
    tp_index = lax.axis_index("tp")
    device_count = dp_count * tp_count
    req_local = cache.shape[0]
    max_len = cache.shape[1]
    latent = cache.shape[2]
    heads_local = query.shape[1]
    value_width = w_uv.shape[1]
    head_width = w_uv.shape[2]
    col_width = w_out.shape[1]
    scale = float(VH + ROPE) ** (-0.5)
    queries = query.reshape(req_local, 2, heads_local, latent)
    fresh = new_latent.reshape(req_local, 2, latent)
    far_score = (
        jnp.einsum("bthc,blc->bthl", queries, cache, preferred_element_type=jnp.float32) * scale
    )
    live = lax.broadcasted_iota(jnp.int32, (req_local, max_len), 1) < cache_len[:, None]
    far_score = jnp.where(live[:, None, None, :], far_score, -jnp.inf)
    near_score = (
        jnp.einsum("bthc,buc->bthu", queries, fresh, preferred_element_type=jnp.float32) * scale
    )
    causal = lax.broadcasted_iota(jnp.int32, (2, 2), 0) >= lax.broadcasted_iota(
        jnp.int32, (2, 2), 1
    )
    near_score = jnp.where(causal[None, :, None, :], near_score, -jnp.inf)
    highest = jnp.maximum(jnp.max(far_score, axis=-1), jnp.max(near_score, axis=-1))[..., None]
    far_weight = jnp.exp(far_score - highest)
    near_weight = jnp.exp(near_score - highest)
    denominator = (jnp.sum(far_weight, axis=-1) + jnp.sum(near_weight, axis=-1))[..., None]
    far_prob = (far_weight / denominator).astype(jnp.bfloat16)
    near_prob = (near_weight / denominator).astype(jnp.bfloat16)
    context = jnp.einsum(
        "bthl,blc->bthc", far_prob, cache[:, :, :value_width], preferred_element_type=jnp.float32
    )
    context = context + jnp.einsum(
        "bthu,buc->bthc", near_prob, fresh[:, :, :value_width], preferred_element_type=jnp.float32
    )
    context = context.astype(jnp.bfloat16).reshape(2 * req_local, heads_local, value_width)
    head_out = jnp.einsum("ihc,hcv->ihv", context, w_uv, preferred_element_type=jnp.float32)
    head_out = head_out.astype(jnp.bfloat16).reshape(2 * req_local, heads_local * head_width)
    partial_out = jnp.dot(
        lax.all_gather(head_out, "dp", axis=0, tiled=True),
        w_out,
        preferred_element_type=jnp.float32,
    )
    attn_part = lax.psum_scatter(partial_out, "tp", scatter_dimension=0, tiled=True)
    mid = hidden_in.astype(jnp.float32) + attn_part
    square_sum = lax.psum(jnp.sum(mid * mid, axis=1), "dp")
    normed = (mid * lax.rsqrt(square_sum / D + EPSILON)[:, None] * norm_gain[None, :]).astype(
        jnp.bfloat16
    )
    quarter = mid.shape[0]
    capacity = 3 * quarter // 4
    row_start = tp_index * quarter
    my_routes = lax.dynamic_slice_in_dim(routing, row_start, quarter, 0)
    my_weights = lax.dynamic_slice_in_dim(route_weight, row_start, quarter, 0)
    expert_ids = lax.broadcasted_iota(jnp.int32, (1, 1, EXPERTS), 2)
    chosen = my_routes[:, :, None] == expert_ids
    member = jnp.sum(chosen.astype(jnp.int32), axis=1).T
    mixing = jnp.sum(jnp.where(chosen, my_weights[:, :, None], 0.0), axis=1).T
    position = jnp.cumsum(member, axis=1) - 1
    slot_ids = lax.broadcasted_iota(jnp.int32, (1, capacity, 1), 1)
    placed = (member[:, None, :] == 1) & (position[:, None, :] == slot_ids)
    dispatch_rows = jnp.einsum(
        "eci,id->ecd", placed.astype(jnp.bfloat16), normed, preferred_element_type=jnp.float32
    ).astype(jnp.bfloat16)
    combine_map = jnp.where(placed, mixing[:, None, :], 0.0)
    device_table = np.arange(device_count) * EXPERTS // device_count
    outgoing = dispatch_rows[device_table]
    arrived = lax.all_to_all(outgoing, ("dp", "tp"), split_axis=0, concat_axis=0, tiled=True)
    full_rows = arrived.reshape(dp_count, tp_count, capacity, col_width).transpose(1, 2, 0, 3)
    full_rows = full_rows.reshape(tp_count * capacity, dp_count * col_width)
    expert_out = expert_block(full_rows, w_gate_up, w_down)
    outgoing_sums = expert_out.reshape(tp_count, capacity, dp_count, col_width).transpose(
        2, 0, 1, 3
    )
    outgoing_sums = outgoing_sums.reshape(device_count, capacity, col_width)
    returned = lax.all_to_all(outgoing_sums, ("dp", "tp"), split_axis=0, concat_axis=0, tiled=True)
    group_size = device_count // EXPERTS
    summed = jnp.sum(returned.reshape(EXPERTS, group_size, capacity, col_width), axis=1)
    moe_out = jnp.einsum("eci,ecd->id", combine_map, summed, precision=lax.Precision.HIGHEST)
    return (mid + moe_out).astype(jnp.bfloat16)


def solution(mesh):
    placed = (
        P("dp", "tp", None),
        P("dp", None),
        P("dp", None, None),
        P("dp"),
        P("tp", None, None),
        P("tp", "dp"),
        P("tp", "dp"),
        P("dp"),
        P(),
        P(),
        P(None, None, ("dp", "tp")),
        P(("dp", "tp"), None),
    )
    return jax.shard_map(
        on_device, mesh=mesh, in_specs=placed, out_specs=P("tp", "dp"), check_vma=False
    )
```

profile of v0, /device:TPU:1, one launch (start us, length us, event | category | flops | bytes accessed | tf_op | source)
XLA Modules:
  0.0 243.6 jit_solution(7760489888673171675)
XLA Ops:
  6.5 0.9 reshape.94
  7.4 0.7 reshape.74
  8.1 0.9 iota_compare_fusion.2
  9.0 2.3 fusion.61
  11.9 0.7 fusion.8
  12.9 0.4 fusion.28
  13.3 26.4 %all-gather = bf16[32,4,2048]{2,1,0:T(4,128)(2,1)S(1)} all-gather(bf16[1,4,2048]{2,1,0:T(4,128)(2,1)S(1)} %fusion.28), channel_id=1, replica_groups=mesh['dp'=32,'tp'=4] {'dp'}, dimensions={0}, use_global_device_ids=true | all-gather | bytes 540672 | tf_op jit(solution)/shard_map/all_gather | solution.py:77
  39.8 2.3 fusion.63
  42.5 18.0 %reduce-scatter.2.cloned.1.call-done = f32[32,224]{1,0:T(8,128)} async-done(((f32[128,224]{1,0:T(8,128)}), f32[32,224]{1,0:T(8,128)}) %reduce-scatter.2.cloned.1.call-update) | async-done | bytes 28688 | tf_op jit(solution)/shard_map/reduce_scatter | solution.py:81
  60.5 0.9 multiply_reduce_fusion
  61.3 65.0 %psum.7 = f32[32]{0:T(128)S(1)} all-reduce(f32[32]{0:T(128)S(1)} %multiply_reduce_fusion), channel_id=1, replica_groups=mesh['dp'=32,'tp'=4] {'dp'}, use_global_device_ids=true, to_apply=%region_9.10 | all-reduce | flops 32 | bytes 256 | tf_op jit(solution)/shard_map/psum | solution.py:83
  126.3 1.0 convolution_convert_fusion
  127.3 1.8 gather_fusion
  129.1 31.7 %all_to_all.10 = bf16[128,24,224]{2,1,0:T(8,128)(2,1)S(1)} all-to-all(bf16[128,24,224]{2,1,0:T(8,128)(2,1)} %gather_fusion), channel_id=1, replica_groups=mesh['dp'=32,'tp'=4] {'dp','tp'}, dimensions={0} | all-to-all | bytes 2752512 | tf_op jit(solution)/shard_map/all_to_all | solution.py:105
  160.8 2.0 copy.43
  162.9 3.4 %reshape.78 = bf16[96,7168]{1,0:T(8,128)(2,1)S(1)} reshape(bf16[4,24,32,224]{3,2,1,0:T(8,128)(2,1)} %bitcast.79) | data formatting | bytes 2752512 | tf_op jit(solution)/shard_map/reshape | solution.py:107
  166.3 3.4 %fusion.2 = f32[96,256]{1,0:T(8,128)} fusion(bf16[96,7168]{1,0:T(8,128)(2,1)S(1)} %reshape.78, bf16[2,7168,256]{2,1,0:T(8,128)(2,1)} %param.24), kind=kOutput, calls=%fused_computation.3 | convolution fusion | flops 352321536 | bytes 5144576 | tf_op jit(solution)/shard_map/dot_general | solution.py:15
  169.7 6.9 %fusion.25 = f32[96,7168]{1,0:T(8,128)} fusion(bf16[256,7168]{1,0:T(8,128)(2,1)} %param.25, bf16[96,7168]{1,0:T(8,128)(2,1)S(1)} %reshape.78, bf16[2,7168,256]{2,1,0:T(8,128)(2,1)} %param.24, f32[96,256]{1,0:T(8,128)} %fusion.2), kind=kOutput, calls=%fused_computation.21 | convolution fusion | flops 704790528 | bytes 11567104 | tf_op jit(solution)/shard_map/dot_general | solution.py:18
  176.6 4.6 %reshape.79 = f32[4,24,32,224]{3,2,1,0:T(8,128)} reshape(f32[96,7168]{1,0:T(8,128)} %fusion.25) | data formatting | bytes 5505024 | tf_op jit(solution)/shard_map/reshape | solution.py:109
  181.2 5.4 %copy.34 = f32[4,24,32,224]{3,1,0,2:T(8,128)} copy(f32[4,24,32,224]{3,2,1,0:T(8,128)} %reshape.79) | data formatting | bytes 5505024 | tf_op jit(solution)/shard_map/reshape | solution.py:109
  186.6 5.0 %all-to-all-start.1 = ((f32[128,24,224]{2,1,0:T(8,128)}), f32[128,24,224]{2,1,0:T(8,128)}, u32[]{:S(2)}, u32[]{:S(2)}) async-start(f32[128,24,224]{2,1,0:T(8,128)} %bitcast.77), calls=%async_computation.2 | async-start | bytes 6291456 | tf_op jit(solution)/shard_map/all_to_all | solution.py:113
  191.7 41.8 %all-to-all-done.1 = f32[128,24,224]{2,1,0:T(8,128)} async-done(((f32[128,24,224]{2,1,0:T(8,128)}), f32[128,24,224]{2,1,0:T(8,128)}, u32[]{:S(2)}, u32[]{:S(2)}) %all-to-all-start.1) | async-done | bytes 2752544 | tf_op jit(solution)/shard_map/all_to_all | solution.py:113
  233.5 2.2 bitcast_reduce_fusion
  235.7 1.1 fusion.29
  (37 shorter events, 1.3 us)
Async XLA Ops:
  6.5 6.3 %copy-start = (bf16[16,512,128]{2,1,0:T(8,128)(2,1)S(1)}, bf16[16,512,128]{2,1,0:T(8,128)(2,1)}, u32[]{:S(2)}) copy-start(bf16[16,512,128]{2,1,0:T(8,128)(2,1)} %param.18) | copy-start | bytes 6291460
  6.5 4.8 %copy-start.4 = (bf16[4,16,576]{2,1,0:T(8,128)(2,1)S(1)}, bf16[4,16,576]{2,1,0:T(8,128)(2,1)}, u32[]{:S(2)}) copy-start(bf16[4,16,576]{2,1,0:T(8,128)(2,1)} %param.14) | copy-start | bytes 221188
  6.5 53.9 %reduce-scatter.2.cloned.1.call-start = ((), (), s32[]{:S(2)}) async-start(), calls=%async_computation.3 | async-start | bytes 163840 | tf_op jit(solution)/shard_map/reduce_scatter | solution.py:81
  8.1 3.7 %copy-start.1 = (bf16[2,1024,576]{1,2,0:T(8,128)(2,1)S(1)}, bf16[2,1024,576]{1,2,0:T(8,128)(2,1)}, u32[]{:S(2)}) copy-start(bf16[2,1024,576]{1,2,0:T(8,128)(2,1)} %param.16) | copy-start | bytes 7077892
  12.8 29.3 %copy-start.5 = (s32[128,8]{0,1:T(8,128)S(1)}, s32[128,8]{0,1:T(8,128)}, u32[]{:S(2)}) copy-start(s32[128,8]{0,1:T(8,128)} %param.22) | copy-start | bytes 12292
  12.8 29.4 %copy-start.8 = (s32[128]{0:T(128)S(1)}, s32[128]{0:T(128)}, u32[]{:S(2)}) copy-start(s32[128]{0:T(128)} %constant.46) | copy-start | bytes 1540
  12.9 47.6 %copy-start.3 = (bf16[32,224]{1,0:T(8,128)(2,1)S(1)}, bf16[32,224]{1,0:T(8,128)(2,1)}, u32[]{:S(2)}) copy-start(bf16[32,224]{1,0:T(8,128)(2,1)} %param.20) | copy-start | bytes 43012
  12.9 113.4 %copy-start.7 = (f32[224]{0:T(256)S(1)}, f32[224]{0:T(256)}, u32[]{:S(2)}) copy-start(f32[224]{0:T(256)} %param.21) | copy-start | bytes 2692
  186.6 5.0 %copy-start.6 = (f32[128,8]{0,1:T(8,128)S(1)}, f32[128,8]{0,1:T(8,128)}, u32[]{:S(2)}) copy-start(f32[128,8]{0,1:T(8,128)} %param.23) | copy-start | bytes 12292
  186.6 46.9 %all-to-all-start.1 = ((f32[128,24,224]{2,1,0:T(8,128)}), f32[128,24,224]{2,1,0:T(8,128)}, u32[]{:S(2)}, u32[]{:S(2)}) async-start(f32[128,24,224]{2,1,0:T(8,128)} %bitcast.77), calls=%async_computation.2 | async-start | bytes 6291456 | tf_op jit(solution)/shard_map/all_to_all | solution.py:113
  191.6 44.1 %copy-start.2 = (f32[32,224]{1,0:T(8,128)S(1)}, f32[32,224]{1,0:T(8,128)}, u32[]{:S(2)}) copy-start(f32[32,224]{1,0:T(8,128)} %reduce-scatter.2.cloned.1.call-done) | copy-start | bytes 86020
Sparse Core Ops, SparseCore 0:
  42.2 18.1 reduce-scatter.1
where the time goes:
time: 244 us
  blocking collectives  123 us (50%)
  waiting for transfers between devices  59.8 us (25%)
  local copies, waits for them, and re-layouts  19.2 us (8%)
  matrix products  18.6 us (8%)
  between operations  13.6 us (6%)
  starting transfers between devices  4.99 us (2%)
  other arithmetic  4.41 us (2%)
    psum x1, blocking collectives, on_device(): square_sum = lax.psum(jnp.sum(mid * mid, axis=1), 'dp')  65 us
    all_to_all x1, waiting for transfers between devices, on_device(): lax.all_to_all(outgoing_sums, ('dp', 'tp'), split_axis=0, concat_axis=0,...  41.8 us
    all_to_all x1, blocking collectives, on_device(): lax.all_to_all(outgoing, ('dp', 'tp'), split_axis=0, concat_axis=0, tiled...  31.7 us
    all_gather x1, blocking collectives, on_device(): lax.all_gather(head_out, 'dp', axis=0, tiled=True)  26.4 us
    reduce_scatter x1, waiting for transfers between devices, on_device(): lax.psum_scatter(partial_out, 'tp', scatter_dimension=0, tiled=True)  18 us
    reshape x2, local copies, waits for them, and re-layouts, on_device(): expert_out.reshape(tp_count, capacity, dp_count, col_width)  10 us
    dot_general x1, matrix products, expert_block(): return jnp.dot(hidden_act, w_down, preferred_element_type=jnp.float32)  6.9 us
    all_to_all x1, starting transfers between devices, on_device(): lax.all_to_all(outgoing_sums, ('dp', 'tp'), split_axis=0, concat_axis=0,...  4.99 us
  transfers between devices with their start and end apart: 2, of which 2 were waited for; matrix products, arithmetic and copies ran while one was open for 0% of the time, Pallas kernels for 0%

commit v1 on v0

--- a/solution.py
+++ b/solution.py
@@ -9,6 +9,18 @@
 VH = 128
 EXPERTS = 16
 EPSILON = 1e-06
+
+
+def doubled_up(x, axis, dim):
+    ways, here, lap = (lax.axis_size(axis), lax.axis_index(axis), x.shape[dim])
+    line, have = (x, 1)
+    while have < ways:
+        line = jnp.concatenate(
+            [line, lax.ppermute(line, axis, [(d, (d - have) % ways) for d in range(ways)])],
+            axis=dim,
+        )
+        have = 2 * have
+    return jnp.roll(line, here * lap, axis=dim)
 
 
 def expert_block(tokens_in, w_gate_up, w_down):
@@ -73,11 +85,7 @@
     context = context.astype(jnp.bfloat16).reshape(2 * req_local, heads_local, value_width)
     head_out = jnp.einsum("ihc,hcv->ihv", context, w_uv, preferred_element_type=jnp.float32)
     head_out = head_out.astype(jnp.bfloat16).reshape(2 * req_local, heads_local * head_width)
-    partial_out = jnp.dot(
-        lax.all_gather(head_out, "dp", axis=0, tiled=True),
-        w_out,
-        preferred_element_type=jnp.float32,
-    )
+    partial_out = jnp.dot(doubled_up(head_out, "dp", 0), w_out, preferred_element_type=jnp.float32)
     attn_part = lax.psum_scatter(partial_out, "tp", scatter_dimension=0, tiled=True)
     mid = hidden_in.astype(jnp.float32) + attn_part
     square_sum = lax.psum(jnp.sum(mid * mid, axis=1), "dp")

time: 244 us -> 257 us (1.053)
  blocking collectives: 123 us -> 96.6 us
  waiting for transfers between devices: 59.8 us -> 84.8 us
  starting transfers between devices: 4.99 us -> 16.5 us
    all_gather x1 -> x0, blocking collectives: 26.4 us -> none  [on_device(): lax.all_gather(head_out, 'dp', axis=0, tiled=True)]
    ppermute x0 -> x5, waiting for transfers between devices: none -> 20.9 us  [doubled_up(): lax.ppermute(line, axis, [(d, (d - have) % ways) for d in range(ways)])]
    ppermute x0 -> x5, starting transfers between devices: none -> 11.5 us  [doubled_up(): lax.ppermute(line, axis, [(d, (d - have) % ways) for d in range(ways)])]
    reduce_scatter x1, waiting for transfers between devices: 18 us -> 22.1 us  [on_device(): lax.psum_scatter(partial_out, 'tp', scatter_dimension=0, tiled=True)]
  transfers between devices with their start and end apart: 2 -> 7, of which waited for: 2 -> 7; matrix products, arithmetic and copies ran while one was open for 0% -> 0% of each run, Pallas kernels for 0% -> 0%
where the time goes in v1:
time: 257 us; the launch traced here: 256 us
  blocking collectives  96.6 us (38%)
  waiting for transfers between devices  84.8 us (33%)
  local copies, waits for them, and re-layouts  21.2 us (8%)
  matrix products  18.6 us (7%)
  starting transfers between devices  16.5 us (6%)
  between operations  13.6 us (5%)
  other arithmetic  4.49 us (2%)
    psum x1, blocking collectives, on_device(): square_sum = lax.psum(jnp.sum(mid * mid, axis=1), 'dp')  65 us
    all_to_all x1, waiting for transfers between devices, on_device(): lax.all_to_all(outgoing_sums, ('dp', 'tp'), split_axis=0, concat_axis=0,...  41.8 us
    all_to_all x1, blocking collectives, on_device(): lax.all_to_all(outgoing, ('dp', 'tp'), split_axis=0, concat_axis=0, tiled...  31.7 us
    reduce_scatter x1, waiting for transfers between devices, on_device(): lax.psum_scatter(partial_out, 'tp', scatter_dimension=0, tiled=True)  22.1 us
    ppermute x5, waiting for transfers between devices, doubled_up(): lax.ppermute(line, axis, [(d, (d - have) % ways) for d in range(ways)])  20.9 us
    ppermute x5, starting transfers between devices, doubled_up(): lax.ppermute(line, axis, [(d, (d - have) % ways) for d in range(ways)])  11.5 us
    reshape x2, local copies, waits for them, and re-layouts, on_device(): expert_out.reshape(tp_count, capacity, dp_count, col_width)  10 us
    dot_general x1, matrix products, expert_block(): return jnp.dot(hidden_act, w_down, preferred_element_type=jnp.float32)  6.9 us
  transfers between devices with their start and end apart: 7, of which 7 were waited for; matrix products, arithmetic and copies ran while one was open for 0% of the time, Pallas kernels for 0%

profile of v1, /device:TPU:1, one launch (start us, length us, event | category | flops | bytes accessed | tf_op | source)
XLA Modules:
  0.0 255.8 jit_solution(14917034849092456208)
XLA Ops:
  9.0 2.3 fusion.64
  13.2 1.5 collective-permute-start
  14.7 2.7 %collective-permute-done = bf16[4,2048]{1,0:T(4,128)(2,1)S(1)} collective-permute-done((bf16[4,2048]{1,0:T(4,128)(2,1)S(1)}, bf16[4,2048]{1,0:T(4,128)(2,1)S(1)}, u32[]{:S(2)}, u32[]{:S(2)}) %collective-permute-start) | collective-permute-done | bytes 16416 | tf_op jit(solution)/shard_map/ppermute | solution.py:19
  17.4 8.2 %collective-permute-start.1 = (bf16[8,2048]{1,0:T(8,128)(2,1)S(1)}, bf16[8,2048]{1,0:T(8,128)(2,1)S(1)}, u32[]{:S(2)}, u32[]{:S(2)}) collective-permute-start(bf16[8,2048]{1,0:T(8,128)(2,1)S(1)} %pad_maximum_fusion.2), channel_id=1, source_target_pairs={{0,120},{4,124},{8,0},{12,4},{16,8},{20,12},{24,16},{28,20},{32,24... | collective-permute-start | bytes 98312 | tf_op jit(solution)/shard_map/ppermute | solution.py:19
  26.7 1.5 collective-permute-start.2
  28.3 3.2 %collective-permute-done.2 = bf16[16,2048]{1,0:T(8,128)(2,1)S(1)} collective-permute-done((bf16[16,2048]{1,0:T(8,128)(2,1)S(1)}, bf16[16,2048]{1,0:T(8,128)(2,1)S(1)}, u32[]{:S(2)}, u32[]{:S(2)}) %collective-permute-start.2) | collective-permute-done | bytes 65568 | tf_op jit(solution)/shard_map/ppermute | solution.py:19
  31.8 5.0 %collective-permute-done.3 = bf16[32,2048]{1,0:T(8,128)(2,1)S(1)} collective-permute-done((bf16[32,2048]{1,0:T(8,128)(2,1)S(1)}, bf16[32,2048]{1,0:T(8,128)(2,1)S(1)}, u32[]{:S(2)}, u32[]{:S(2)}) %collective-permute-start.3) | collective-permute-done | bytes 131104 | tf_op jit(solution)/shard_map/ppermute | solution.py:19
  36.9 9.0 %collective-permute-done.4 = bf16[64,2048]{1,0:T(8,128)(2,1)} collective-permute-done((bf16[64,2048]{1,0:T(8,128)(2,1)S(1)}, bf16[64,2048]{1,0:T(8,128)(2,1)}, u32[]{:S(2)}, u32[]{:S(2)}) %collective-permute-start.4) | collective-permute-done | bytes 262176 | tf_op jit(solution)/shard_map/ppermute | solution.py:19
  46.0 2.1 concatenate.26
  48.1 2.3 fusion.31
  50.6 22.1 %reduce-scatter.2.cloned.1.call-done = f32[32,224]{1,0:T(8,128)} async-done(((f32[128,224]{1,0:T(8,128)}), f32[32,224]{1,0:T(8,128)}) %reduce-scatter.2.cloned.1.call-update) | async-done | bytes 28688 | tf_op jit(solution)/shard_map/reduce_scatter | solution.py:89
  73.5 65.0 %psum.7 = f32[32]{0:T(128)S(1)} all-reduce(f32[32]{0:T(128)S(1)} %multiply_reduce_fusion), channel_id=1, replica_groups=mesh['dp'=32,'tp'=4] {'dp'}, use_global_device_ids=true, to_apply=%region_9.10 | all-reduce | flops 32 | bytes 256 | tf_op jit(solution)/shard_map/psum | solution.py:91
  139.5 1.8 gather_fusion
  141.3 31.7 %all_to_all.10 = bf16[128,24,224]{2,1,0:T(8,128)(2,1)S(1)} all-to-all(bf16[128,24,224]{2,1,0:T(8,128)(2,1)} %gather_fusion), channel_id=1, replica_groups=mesh['dp'=32,'tp'=4] {'dp','tp'}, dimensions={0} | all-to-all | bytes 2752512 | tf_op jit(solution)/shard_map/all_to_all | solution.py:113
  173.0 2.0 copy.37
  175.1 3.4 %reshape.78 = bf16[96,7168]{1,0:T(8,128)(2,1)S(1)} reshape(bf16[4,24,32,224]{3,2,1,0:T(8,128)(2,1)} %bitcast.78) | data formatting | bytes 2752512 | tf_op jit(solution)/shard_map/reshape | solution.py:115
  178.5 3.4 %fusion.2 = f32[96,256]{1,0:T(8,128)} fusion(bf16[96,7168]{1,0:T(8,128)(2,1)S(1)} %reshape.78, bf16[2,7168,256]{2,1,0:T(8,128)(2,1)} %param.24), kind=kOutput, calls=%fused_computation.3 | convolution fusion | flops 352321536 | bytes 5144576 | tf_op jit(solution)/shard_map/dot_general | solution.py:27
  181.9 6.9 %fusion.25 = f32[96,7168]{1,0:T(8,128)} fusion(bf16[256,7168]{1,0:T(8,128)(2,1)} %param.25, bf16[96,7168]{1,0:T(8,128)(2,1)S(1)} %reshape.78, bf16[2,7168,256]{2,1,0:T(8,128)(2,1)} %param.24, f32[96,256]{1,0:T(8,128)} %fusion.2), kind=kOutput, calls=%fused_computation.21 | convolution fusion | flops 704790528 | bytes 11567104 | tf_op jit(solution)/shard_map/dot_general | solution.py:30
  188.8 4.6 %reshape.79 = f32[4,24,32,224]{3,2,1,0:T(8,128)} reshape(f32[96,7168]{1,0:T(8,128)} %fusion.25) | data formatting | bytes 5505024 | tf_op jit(solution)/shard_map/reshape | solution.py:117
  193.4 5.4 %copy.28 = f32[4,24,32,224]{3,1,0,2:T(8,128)} copy(f32[4,24,32,224]{3,2,1,0:T(8,128)} %reshape.79) | data formatting | bytes 5505024 | tf_op jit(solution)/shard_map/reshape | solution.py:117
  198.8 5.0 %all-to-all-start.1 = ((f32[128,24,224]{2,1,0:T(8,128)}), f32[128,24,224]{2,1,0:T(8,128)}, u32[]{:S(2)}, u32[]{:S(2)}) async-start(f32[128,24,224]{2,1,0:T(8,128)} %bitcast.76), calls=%async_computation.2 | async-start | bytes 6291456 | tf_op jit(solution)/shard_map/all_to_all | solution.py:121
  203.9 41.8 %all-to-all-done.1 = f32[128,24,224]{2,1,0:T(8,128)} async-done(((f32[128,24,224]{2,1,0:T(8,128)}), f32[128,24,224]{2,1,0:T(8,128)}, u32[]{:S(2)}, u32[]{:S(2)}) %all-to-all-start.1) | async-done | bytes 2752544 | tf_op jit(solution)/shard_map/all_to_all | solution.py:121
  245.7 2.2 bitcast_reduce_fusion
  247.9 1.1 fusion.29
  (50 shorter events, 8.1 us)
Async XLA Ops:
  6.5 6.3 %copy-start = (bf16[16,512,128]{2,1,0:T(8,128)(2,1)S(1)}, bf16[16,512,128]{2,1,0:T(8,128)(2,1)}, u32[]{:S(2)}) copy-start(bf16[16,512,128]{2,1,0:T(8,128)(2,1)} %param.18) | copy-start | bytes 6291460
  6.5 4.8 %copy-start.4 = (bf16[4,16,576]{2,1,0:T(8,128)(2,1)S(1)}, bf16[4,16,576]{2,1,0:T(8,128)(2,1)}, u32[]{:S(2)}) copy-start(bf16[4,16,576]{2,1,0:T(8,128)(2,1)} %param.14) | copy-start | bytes 221188
  6.5 66.1 %reduce-scatter.2.cloned.1.call-start = ((), (), s32[]{:S(2)}) async-start(), calls=%async_computation.3 | async-start | bytes 163840 | tf_op jit(solution)/shard_map/reduce_scatter | solution.py:89
  8.1 3.7 %copy-start.1 = (bf16[2,1024,576]{1,2,0:T(8,128)(2,1)S(1)}, bf16[2,1024,576]{1,2,0:T(8,128)(2,1)}, u32[]{:S(2)}) copy-start(bf16[2,1024,576]{1,2,0:T(8,128)(2,1)} %param.16) | copy-start | bytes 7077892
  11.9 19.8 %copy-start.5 = (s32[128,8]{0,1:T(8,128)S(1)}, s32[128,8]{0,1:T(8,128)}, u32[]{:S(2)}) copy-start(s32[128,8]{0,1:T(8,128)} %param.22) | copy-start | bytes 12292
  13.2 4.2 %collective-permute-start = (bf16[4,2048]{1,0:T(4,128)(2,1)S(1)}, bf16[4,2048]{1,0:T(4,128)(2,1)S(1)}, u32[]{:S(2)}, u32[]{:S(2)}) collective-permute-start(bf16[4,2048]{1,0:T(4,128)(2,1)S(1)} %fusion.28), channel_id=1, source_target_pairs={{0,124},{4,0},{8,4},{12,8},{16,12},{20,16},{24,20},{28,24},{32,28}... | collective-permute-start | bytes 49160 | tf_op jit(solution)/shard_map/ppermute | solution.py:19
  17.4 9.2 %collective-permute-start.1 = (bf16[8,2048]{1,0:T(8,128)(2,1)S(1)}, bf16[8,2048]{1,0:T(8,128)(2,1)S(1)}, u32[]{:S(2)}, u32[]{:S(2)}) collective-permute-start(bf16[8,2048]{1,0:T(8,128)(2,1)S(1)} %pad_maximum_fusion.2), channel_id=1, source_target_pairs={{0,120},{4,124},{8,0},{12,4},{16,8},{20,12},{24,16},{28,20},{32,24... | collective-permute-start | bytes 98312 | tf_op jit(solution)/shard_map/ppermute | solution.py:19
  26.7 23.7 %copy-start.8 = (s32[128]{0:T(128)S(1)}, s32[128]{0:T(128)}, u32[]{:S(2)}) copy-start(s32[128]{0:T(128)} %constant.73) | copy-start | bytes 1540
  26.7 46.0 %copy-start.3 = (bf16[32,224]{1,0:T(8,128)(2,1)S(1)}, bf16[32,224]{1,0:T(8,128)(2,1)}, u32[]{:S(2)}) copy-start(bf16[32,224]{1,0:T(8,128)(2,1)} %param.20) | copy-start | bytes 43012
  26.7 111.8 %copy-start.7 = (f32[224]{0:T(256)S(1)}, f32[224]{0:T(256)}, u32[]{:S(2)}) copy-start(f32[224]{0:T(256)} %param.21) | copy-start | bytes 2692
  26.7 4.7 %collective-permute-start.2 = (bf16[16,2048]{1,0:T(8,128)(2,1)S(1)}, bf16[16,2048]{1,0:T(8,128)(2,1)S(1)}, u32[]{:S(2)}, u32[]{:S(2)}) collective-permute-start(bf16[16,2048]{1,0:T(8,128)(2,1)S(1)} %pad_maximum_fusion.1), channel_id=1, source_target_pairs={{0,112},{4,116},{8,120},{12,124},{16,0},{20,4},{24,8},{28,12},{32,... | collective-permute-start | bytes 196616 | tf_op jit(solution)/shard_map/ppermute | solution.py:19
  31.5 5.3 %collective-permute-start.3 = (bf16[32,2048]{1,0:T(8,128)(2,1)S(1)}, bf16[32,2048]{1,0:T(8,128)(2,1)S(1)}, u32[]{:S(2)}, u32[]{:S(2)}) collective-permute-start(bf16[32,2048]{1,0:T(8,128)(2,1)S(1)} %pad_maximum_fusion), channel_id=1, source_target_pairs={{0,96},{4,100},{8,104},{12,108},{16,112},{20,116},{24,120},{28,124... | collective-permute-start | bytes 393224 | tf_op jit(solution)/shard_map/ppermute | solution.py:19
  36.8 9.2 %collective-permute-start.4 = (bf16[64,2048]{1,0:T(8,128)(2,1)S(1)}, bf16[64,2048]{1,0:T(8,128)(2,1)}, u32[]{:S(2)}, u32[]{:S(2)}) collective-permute-start(bf16[64,2048]{1,0:T(8,128)(2,1)S(1)} %concatenate.25), channel_id=1, source_target_pairs={{0,64},{4,68},{8,72},{12,76},{16,80},{20,84},{24,88},{28,92},{32,9... | collective-permute-start | bytes 786440 | tf_op jit(solution)/shard_map/ppermute | solution.py:19
  198.8 5.0 %copy-start.6 = (f32[128,8]{0,1:T(8,128)S(1)}, f32[128,8]{0,1:T(8,128)}, u32[]{:S(2)}) copy-start(f32[128,8]{0,1:T(8,128)} %param.23) | copy-start | bytes 12292
  198.8 46.9 %all-to-all-start.1 = ((f32[128,24,224]{2,1,0:T(8,128)}), f32[128,24,224]{2,1,0:T(8,128)}, u32[]{:S(2)}, u32[]{:S(2)}) async-start(f32[128,24,224]{2,1,0:T(8,128)} %bitcast.76), calls=%async_computation.2 | async-start | bytes 6291456 | tf_op jit(solution)/shard_map/all_to_all | solution.py:121
  203.8 44.1 %copy-start.2 = (f32[32,224]{1,0:T(8,128)S(1)}, f32[32,224]{1,0:T(8,128)}, u32[]{:S(2)}) copy-start(f32[32,224]{1,0:T(8,128)} %reduce-scatter.2.cloned.1.call-done) | copy-start | bytes 86020
Sparse Core Ops, SparseCore 0:
  50.5 22.1 reduce-scatter.1
